TPU v7x, 32 devices: a whole 2x2x4 slice. The times are simulated.
32 devices in a mesh: dp: 4 (over y, core), expert: 2 (over x), tensor: 4 (over z).
Axes of the slice: x: 2, y: 2, z: 4, core: 2. Of those that a mesh axis runs over, the one named last changes fastest.
Arguments:
- tokens: bfloat16 [16, 1024, 768], P(('dp', 'expert')), may hold values from -6 to 6
- segments: int32 [16, 1024], P(('dp', 'expert')), may hold values from 0 to 3, never falling along the last dimension, each value on 1 to 512 neighbouring positions
- routes: int32 [16, 1024, 1], P(('dp', 'expert')), may hold values from 0 to 1; in each aligned block of 2048 rows (0 to 2047, 2048 to 4095, ..., all dimensions but the last counted through in order) at most 1280 rows name the same one
- rel_bucket: int32 [2047], replicated, may hold values from 0 to 31, as said below
- norm1_gain: bfloat16 [768], replicated, may hold values from 0.5 to 1.5
- query_key_value_weight: bfloat16 [768, 3, 768], P(None, None, 'tensor'), may hold values from -0.21875 to 0.21875
- output_weight: bfloat16 [768, 768], P(None, 'tensor'), may hold values from -3.5 to 3.5
- bias_table: bfloat16 [32, 12], P(None, 'tensor'), may hold values from -4 to 4
- norm2_gain: bfloat16 [768], replicated, may hold values from 0.5 to 1.5
- w_router: bfloat16 [768, 2], replicated, may hold values from -0.109375 to 0.109375
- w_in: bfloat16 [2, 768, 3072], P('expert', None, 'tensor'), may hold values from -0.21875 to 0.21875
- w_expert_out: bfloat16 [2, 768, 3072], P('expert', None, 'tensor'), may hold values from -0.21875 to 0.21875
- cotangent: bfloat16 [16, 1024, 768], P(('dp', 'expert')), may hold values from -6 to 6
Outputs:
- output: bfloat16 [16, 1024, 768], P(('dp', 'expert'))
- input_grad: bfloat16 [16, 1024, 768], P(('dp', 'expert'))
- grad_norm1: float32 [768], P(('dp', 'expert'))
- grad_qkv: float32 [768, 3, 768], P(('dp', 'expert'), None, 'tensor')
- grad_out: float32 [768, 768], P(('dp', 'expert'), 'tensor')
- grad_table: float32 [32, 12], P(None, 'tensor')
- grad_norm2: float32 [768], P(('dp', 'expert'))
- grad_router: float32 [768, 2], P(('dp', 'expert'))
- grad_in: float32 [2, 768, 3072], P('expert', 'dp', 'tensor')
- grad_expert_out: float32 [2, 768, 3072], P('expert', 'dp', 'tensor')
Inputs may be any that keep to these rules, and one draw needn't show every extreme that they name: `routes`: in the 2048 tokens of one device (aligned blocks) no expert is named by more than 1280 tokens, a bound that some block reaches. `segments`: never falls along a sequence; each document has 1 to 512 tokens. `rel_bucket`: offsets r <= 0 take buckets 0 to 15 and offsets r > 0 buckets 16 to 31; within each sign the bucket never falls as |r| grows and equals |r| (plus 16 for r > 0) for |r| < 8.
All inputs are finite; a program needn't handle non-finite values.
Results may differ from a plain program's by a relative error of at most 0.017.
Values may be sent and summed in bfloat16 or wider, within the bound.
A program may use at most 192 MiB of HBM per device.

v0:
```python
import math

import jax
import jax.numpy as jnp
from jax import lax
from jax.sharding import PartitionSpec as P

HIGHEST_PRECISE = lax.Precision.HIGHEST


def smooth(values_in):
    return (
        0.5
        * values_in
        * (
            1.0
            + jnp.tanh(
                0.7978845608028654 * (values_in + 0.044715 * values_in * values_in * values_in)
            )
        )
    )


def normed(values_in, gain_vec):
    return (
        values_in
        * lax.rsqrt(jnp.mean(values_in * values_in, axis=-1, keepdims=True) + 1e-06)
        * gain_vec
    )


def bias_block(rel_bias, start, block_rows, length):
    heads_here = rel_bias.shape[0]
    window = lax.dynamic_slice_in_dim(
        rel_bias, length - start - block_rows, length + block_rows - 1, 1
    )
    widened = jnp.pad(window, ((0, 0), (0, 1)))
    row_len = length + block_rows + 1
    tiled = jnp.tile(widened, (1, block_rows + 1))[:, : block_rows * row_len]
    shifted = tiled.reshape(heads_here, block_rows, row_len)[:, :, :length]
    return shifted[:, ::-1, :]


def per_device(
    tokens,
    segments,
    routes,
    rel_bucket,
    norm1_gain,
    query_key_value_weight,
    output_weight,
    bias_table,
    norm2_gain,
    w_router,
    w_in,
    w_expert_out,
    cotangent,
):
    seq_count, length, model_width = tokens.shape
    tok_count = seq_count * length
    heads_here = bias_table.shape[1]
    bucket_count = bias_table.shape[0]
    head_feat = query_key_value_weight.shape[2]
    head_size = head_feat // heads_here
    experts = w_router.shape[1]
    local_exp = w_in.shape[0]
    sources = experts // local_exp
    capacity = tok_count * 5 // (4 * experts)
    share_slots = capacity // lax.axis_size("tensor")
    slot_start = lax.axis_index("tensor") * share_slots
    block_rows = min(512, length)
    block_count = length // block_rows
    score_scale = 1.0 / math.sqrt(head_size)
    inputs_f = tokens.reshape(tok_count, model_width).astype(jnp.float32)
    gain_one = norm1_gain.astype(jnp.float32)
    gain_two = norm2_gain.astype(jnp.float32)
    attention_input = normed(inputs_f, gain_one).astype(jnp.bfloat16)
    query_key_value = jnp.einsum(
        "td,dcf->tcf", attention_input, query_key_value_weight, preferred_element_type=jnp.float32
    ).astype(jnp.bfloat16)
    queries = query_key_value[:, 0].reshape(seq_count, length, heads_here, head_size)
    keys = query_key_value[:, 1].reshape(seq_count, length, heads_here, head_size)
    values = query_key_value[:, 2].reshape(seq_count, length, heads_here, head_size)
    bucket_hot = (rel_bucket[:, None] == jnp.arange(bucket_count, dtype=jnp.int32)[None, :]).astype(
        jnp.float32
    )
    rel_bias = jnp.dot(bucket_hot, bias_table.astype(jnp.float32), precision=HIGHEST_PRECISE).T

    def scores_of(start):
        query_blk = lax.dynamic_slice_in_dim(queries, start, block_rows, 1)
        seg_blk = lax.dynamic_slice_in_dim(segments, start, block_rows, 1)
        bias_blk = bias_block(rel_bias, start, block_rows, length)
        raw_scores = (
            jnp.einsum("sqhd,skhd->shqk", query_blk, keys, preferred_element_type=jnp.float32)
            * score_scale
            + bias_blk[None]
        )
        same_doc = (seg_blk[:, :, None] == segments[:, None, :])[:, None]
        return (jnp.where(same_doc, raw_scores, -1e30), query_blk)

    def forward_block(start):
        masked, query_blk = scores_of(start)
        row_max = jnp.max(masked, axis=-1, keepdims=True)
        exp_scores = jnp.exp(masked - row_max)
        row_total = jnp.sum(exp_scores, axis=-1, keepdims=True)
        prob_blk = (exp_scores / row_total).astype(jnp.bfloat16)
        mixed_blk = jnp.einsum(
            "shqk,skhd->sqhd", prob_blk, values, preferred_element_type=jnp.float32
        ).astype(jnp.bfloat16)
        return (mixed_blk, (row_max + jnp.log(row_total))[..., 0])

    starts = jnp.arange(block_count, dtype=jnp.int32) * block_rows
    mixed_all, log_totals = lax.map(forward_block, starts)
    attn_rows = jnp.moveaxis(mixed_all, 0, 1).reshape(tok_count, head_feat)
    attn_part = jnp.einsum(
        "tf,df->td", attn_rows, output_weight, preferred_element_type=jnp.float32
    )
    attn_total = lax.psum(attn_part, "tensor")
    residual = inputs_f + attn_total
    moe_in = normed(residual, gain_two).astype(jnp.bfloat16)
    router_f = w_router.astype(jnp.float32)
    route_flat = routes.reshape(tok_count)
    chosen = (route_flat[:, None] == jnp.arange(experts, dtype=jnp.int32)[None, :]).astype(
        jnp.float32
    )

    def gate_of(rows_in, router_in):
        logits = jnp.dot(rows_in, router_in, precision=HIGHEST_PRECISE)
        return jnp.sum(jax.nn.softmax(logits, axis=-1) * chosen, axis=-1)

    gate_value, gate_back = jax.vjp(gate_of, moe_in.astype(jnp.float32), router_f)
    tok_pos = jnp.arange(tok_count, dtype=jnp.int32)
    earlier = (tok_pos[:, None] > tok_pos[None, :]).astype(jnp.bfloat16)
    before_count = jnp.dot(earlier, chosen.astype(jnp.bfloat16), preferred_element_type=jnp.float32)
    slot_rank = jnp.sum(before_count * chosen, axis=1).astype(jnp.int32)
    flat_place = route_flat * capacity + slot_rank
    place_hot = (
        flat_place[:, None] == jnp.arange(experts * capacity, dtype=jnp.int32)[None, :]
    ).astype(jnp.bfloat16)

    def to_slots(rows_tok):
        return (
            jnp.einsum("tp,td->pd", place_hot, rows_tok, preferred_element_type=jnp.float32)
            .astype(jnp.bfloat16)
            .reshape(experts, capacity, model_width)
        )

    def from_slots(rows_slot):
        return jnp.einsum(
            "tp,pd->td",
            place_hot,
            rows_slot.reshape(experts * capacity, model_width),
            preferred_element_type=jnp.float32,
        )

    send_rows = to_slots(moe_in)
    part_in = lax.all_to_all(
        lax.dynamic_slice_in_dim(send_rows, slot_start, share_slots, 1),
        "expert",
        split_axis=0,
        concat_axis=0,
        tiled=True,
    )
    expert_in = lax.all_gather(part_in, "tensor", axis=1, tiled=True)
    expert_in = expert_in.reshape(sources, local_exp, capacity, model_width)
    hidden = jnp.einsum("slcd,ldf->slcf", expert_in, w_in, preferred_element_type=jnp.float32)
    active = smooth(hidden).astype(jnp.bfloat16)
    out_part = jnp.einsum(
        "slcf,ldf->slcd", active, w_expert_out, preferred_element_type=jnp.float32
    )
    shares = lax.psum_scatter(out_part, "tensor", scatter_dimension=2, tiled=True).astype(
        jnp.bfloat16
    )
    back_part = lax.all_to_all(
        shares.reshape(experts, share_slots, model_width),
        "expert",
        split_axis=0,
        concat_axis=0,
        tiled=True,
    )
    returned = lax.all_gather(back_part, "tensor", axis=1, tiled=True)
    expert_rows = from_slots(returned)
    combined = residual + gate_value[:, None] * expert_rows
    output = combined.astype(jnp.bfloat16).reshape(tokens.shape)
    grad_output = cotangent.reshape(tok_count, model_width).astype(jnp.float32)
    d_gate = jnp.sum(grad_output * expert_rows, axis=-1)
    d_rows_tok = (gate_value[:, None] * grad_output).astype(jnp.bfloat16)
    d_router_in, d_router = gate_back(d_gate)
    send_grad = to_slots(d_rows_tok)
    grad_share = lax.all_to_all(
        lax.dynamic_slice_in_dim(send_grad, slot_start, share_slots, 1),
        "expert",
        split_axis=0,
        concat_axis=0,
        tiled=True,
    )
    grad_rows = lax.all_gather(grad_share, "tensor", axis=1, tiled=True)
    grad_rows = grad_rows.reshape(sources, local_exp, capacity, model_width)
    d_active = jnp.einsum(
        "slcd,ldf->slcf", grad_rows, w_expert_out, preferred_element_type=jnp.float32
    )
    smooth_back = jax.vjp(smooth, hidden)[1]
    d_hidden = smooth_back(d_active)[0].astype(jnp.bfloat16)
    grad_w_eout = jnp.einsum(
        "slcd,slcf->ldf", grad_rows, active, preferred_element_type=jnp.float32
    )
    grad_w_in = jnp.einsum(
        "slcd,slcf->ldf", expert_in, d_hidden, preferred_element_type=jnp.float32
    )
    row_part = jnp.einsum("slcf,ldf->slcd", d_hidden, w_in, preferred_element_type=jnp.float32)
    row_share = lax.psum_scatter(row_part, "tensor", scatter_dimension=2, tiled=True).astype(
        jnp.bfloat16
    )
    row_home = lax.all_to_all(
        row_share.reshape(experts, share_slots, model_width),
        "expert",
        split_axis=0,
        concat_axis=0,
        tiled=True,
    )
    row_back = lax.all_gather(row_home, "tensor", axis=1, tiled=True)
    d_moe = from_slots(row_back) + d_router_in
    norm_two_back = jax.vjp(normed, residual, gain_two)[1]
    d_resid_norm, d_gain_two = norm_two_back(d_moe)
    d_residual = grad_output + d_resid_norm
    d_attn_out = d_residual.astype(jnp.bfloat16)
    grad_w_out = jnp.einsum("td,tf->df", d_attn_out, attn_rows, preferred_element_type=jnp.float32)
    d_mixed = jnp.einsum(
        "td,df->tf", d_attn_out, output_weight, preferred_element_type=jnp.float32
    ).astype(jnp.bfloat16)
    d_mixed = d_mixed.reshape(seq_count, length, heads_here, head_size)
    diag_width = length + block_rows - 1

    def backward_block(carry, item):
        d_keys, d_values, d_rel = carry
        start, log_total = item
        masked, query_blk = scores_of(start)
        prob_blk = jnp.exp(masked - log_total[..., None])
        grad_blk = lax.dynamic_slice_in_dim(d_mixed, start, block_rows, 1)
        d_probs = jnp.einsum(
            "sqhd,skhd->shqk", grad_blk, values, preferred_element_type=jnp.float32
        )
        d_scores = (
            prob_blk * (d_probs - jnp.sum(prob_blk * d_probs, axis=-1, keepdims=True))
        ).astype(jnp.bfloat16)
        d_query = (
            jnp.einsum("shqk,skhd->sqhd", d_scores, keys, preferred_element_type=jnp.float32)
            * score_scale
        )
        d_keys = (
            d_keys
            + jnp.einsum("shqk,sqhd->skhd", d_scores, query_blk, preferred_element_type=jnp.float32)
            * score_scale
        )
        d_values = d_values + jnp.einsum(
            "shqk,sqhd->skhd",
            prob_blk.astype(jnp.bfloat16),
            grad_blk,
            preferred_element_type=jnp.float32,
        )
        head_sums = jnp.sum(d_scores.astype(jnp.float32), axis=0)[:, ::-1, :]
        padded = jnp.pad(head_sums, ((0, 0), (0, 0), (0, block_rows + 1)))
        skewed = padded.reshape(heads_here, -1)[:, : block_rows * (length + block_rows)]
        diagonal = jnp.sum(skewed.reshape(heads_here, block_rows, length + block_rows), axis=1)[
            :, :diag_width
        ]
        offset = length - block_rows - start
        window = lax.dynamic_slice_in_dim(d_rel, offset, diag_width, 1) + diagonal
        d_rel = lax.dynamic_update_slice_in_dim(d_rel, window, offset, 1)
        return ((d_keys, d_values, d_rel), d_query.astype(jnp.bfloat16))

    zero_kv = jnp.zeros((seq_count, length, heads_here, head_size), jnp.float32)
    zero_rel = jnp.zeros((heads_here, 2 * length - 1), jnp.float32)
    (d_keys, d_values, d_rel), d_queries = lax.scan(
        backward_block, (zero_kv, zero_kv, zero_rel), (starts, log_totals)
    )
    d_queries = jnp.moveaxis(d_queries, 0, 1).reshape(tok_count, head_feat)
    d_qkv = jnp.stack(
        [
            d_queries,
            d_keys.astype(jnp.bfloat16).reshape(tok_count, head_feat),
            d_values.astype(jnp.bfloat16).reshape(tok_count, head_feat),
        ],
        axis=1,
    )
    grad_w_qkv = jnp.einsum(
        "td,tcf->dcf", attention_input, d_qkv, preferred_element_type=jnp.float32
    )
    d_in_part = jnp.einsum(
        "tcf,dcf->td", d_qkv, query_key_value_weight, preferred_element_type=jnp.float32
    )
    d_in_total = lax.psum(d_in_part.astype(jnp.bfloat16), "tensor").astype(jnp.float32)
    norm_one_back = jax.vjp(normed, inputs_f, gain_one)[1]
    d_inputs, d_gain_one = norm_one_back(d_in_total)
    input_grad = (d_inputs + d_residual).astype(jnp.bfloat16).reshape(tokens.shape)
    grad_table = jnp.dot(bucket_hot.T, d_rel.T, precision=HIGHEST_PRECISE)
    dense = (
        lax.psum_scatter(d_gain_one, ("dp", "expert"), scatter_dimension=0, tiled=True),
        lax.psum_scatter(grad_w_qkv, ("dp", "expert"), scatter_dimension=0, tiled=True),
        lax.psum_scatter(grad_w_out, ("dp", "expert"), scatter_dimension=0, tiled=True),
        lax.psum_scatter(d_router, ("dp", "expert"), scatter_dimension=0, tiled=True),
        lax.psum_scatter(d_gain_two, ("dp", "expert"), scatter_dimension=0, tiled=True),
    )
    table_total = lax.psum(grad_table, ("dp", "expert"))
    expert_total = (
        lax.psum_scatter(
            grad_w_in.astype(jnp.bfloat16), "dp", scatter_dimension=1, tiled=True
        ).astype(jnp.float32),
        lax.psum_scatter(
            grad_w_eout.astype(jnp.bfloat16), "dp", scatter_dimension=1, tiled=True
        ).astype(jnp.float32),
    )
    return (
        output,
        input_grad,
        dense[0],
        dense[1],
        dense[2],
        table_total,
        dense[4],
        dense[3],
        expert_total[0],
        expert_total[1],
    )


def solution(mesh):
    placed = (
        P(("dp", "expert"), None, None),
        P(("dp", "expert"), None),
        P(("dp", "expert"), None, None),
        P(),
        P(),
        P(None, None, "tensor"),
        P(None, "tensor"),
        P(None, "tensor"),
        P(),
        P(),
        P("expert", None, "tensor"),
        P("expert", None, "tensor"),
        P(("dp", "expert"), None, None),
    )
    return jax.shard_map(
        per_device,
        mesh=mesh,
        in_specs=placed,
        out_specs=(
            P(("dp", "expert"), None, None),
            P(("dp", "expert"), None, None),
            P(("dp", "expert")),
            P(("dp", "expert"), None, "tensor"),
            P(("dp", "expert"), "tensor"),
            P(None, "tensor"),
            P(("dp", "expert")),
            P(("dp", "expert"), None),
            P("expert", "dp", "tensor"),
            P("expert", "dp", "tensor"),
        ),
        check_vma=False,
    )
```

profile of v0, /device:TPU:0, one launch (start us, length us, event | category | flops | bytes accessed | tf_op | source)
XLA Modules:
  0.0 2033.8 jit_solution(11616121628838192361)
XLA Ops:
  29.2 281.6 %while.37 = (s32[]{:T(128)}, bf16[2,2,512,3,64]{2,4,3,1,0:T(8,128)(2,1)}, f32[2,2,3,512]{3,2,1,0:T(4,128)}, s32[2]{0:T(128)S(1)}, s32[2,1024]{1,0:T(2,128)S(1)},...) while((s32[]{:T(128)}, ...), condition=%wide.region_4.5_spmd, body=%wide.region_1.4_spmd.sunk | while | flops 853734400 | bytes 202944784 | solution.py:113
  37.0 21.8 %copy.81 = f32[1,3,513,1536]{3,1,2,0:T(4,128)S(1)} copy(f32[1,3,513,1536]{3,2,1,0:T(8,128)S(1)} %broadcast_bitcast_fusion.4) | data formatting | bytes 18911232 | tf_op jit(solution)/shard_map/while
  99.9 48.5 %rev.32 = f32[3,512,1024]{2,1,0:T(8,128)} reverse(f32[3,512,1024]{2,1,0:T(8,128)} %slice.90), dimensions={1} | reverse | bytes 12582912 | tf_op jit(solution)/shard_map/while/body/eval_jaxpr/rev | solution.py:41
  173.7 21.8 %copy.81 = f32[1,3,513,1536]{3,1,2,0:T(4,128)S(1)} copy(f32[1,3,513,1536]{3,2,1,0:T(8,128)S(1)} %broadcast_bitcast_fusion.4) | data formatting | bytes 18911232 | tf_op jit(solution)/shard_map/while
  236.6 48.5 %rev.32 = f32[3,512,1024]{2,1,0:T(8,128)} reverse(f32[3,512,1024]{2,1,0:T(8,128)} %slice.90), dimensions={1} | reverse | bytes 12582912 | tf_op jit(solution)/shard_map/while/body/eval_jaxpr/rev | solution.py:41
  323.0 224.1 %all-reduce.9.cloned.1.call-done = f32[2048,768]{1,0:T(8,128)} async-done(((f32[2048,768]{1,0:T(8,128)}), f32[2048,768]{1,0:T(8,128)}) %all-reduce.9.cloned.1.call-update) | async-done | bytes 6291472 | tf_op jit(solution)/shard_map/psum | solution.py:118
  579.8 74.3 %all-gather.5.cloned.1.call-done = bf16[2,1280,768]{2,1,0:T(8,128)(2,1)} async-done(((bf16[2,320,768]{2,1,0:T(8,128)(2,1)}), bf16[2,1280,768]{2,1,0:T(8,128)(2,1)}) %all-gather.5.cloned.1.call-update) | async-done | bytes 3932176 | tf_op jit(solution)/shard_map/all_gather | solution.py:164
  669.6 134.9 %reduce-scatter.10.cloned.1.call-done = f32[2,1,320,768]{3,2,0,1:T(8,128)} async-done(((f32[2,1,1280,768]{3,2,0,1:T(8,128)}), f32[2,1,320,768]{3,2,0,1:T(8,128)}) %reduce-scatter.10.cloned.1.call-update) | async-done | bytes 1966096 | tf_op jit(solution)/shard_map/reduce_scatter | solution.py:171
  825.6 73.3 %all-gather.7.cloned.1.call-done = bf16[2,1280,768]{2,1,0:T(8,128)(2,1)} async-done(((bf16[2,320,768]{2,1,0:T(8,128)(2,1)}), bf16[2,1280,768]{2,1,0:T(8,128)(2,1)}) %all-gather.7.cloned.1.call-update) | async-done | bytes 3932176 | tf_op jit(solution)/shard_map/all_gather | solution.py:181
  940.5 74.1 %all-gather.9.cloned.1.call-done = bf16[2,1280,768]{2,1,0:T(8,128)(2,1)} async-done(((bf16[2,320,768]{2,1,0:T(8,128)(2,1)}), bf16[2,1280,768]{2,1,0:T(8,128)(2,1)}) %all-gather.9.cloned.1.call-update) | async-done | bytes 3932176 | tf_op jit(solution)/shard_map/all_gather | solution.py:197
  1033.6 134.9 %reduce-scatter.12.cloned.1.call-done = f32[2,1,320,768]{3,2,0,1:T(8,128)} async-done(((f32[2,1,1280,768]{3,2,0,1:T(8,128)}), f32[2,1,320,768]{3,2,0,1:T(8,128)}) %reduce-scatter.12.cloned.1.call-update) | async-done | bytes 1966096 | tf_op jit(solution)/shard_map/reduce_scatter | solution.py:211
  1210.6 52.2 %all-gather.11.cloned.1.call-done = bf16[2,1280,768]{2,1,0:T(8,128)(2,1)} async-done(((bf16[2,320,768]{2,1,0:T(8,128)(2,1)}), bf16[2,1280,768]{2,1,0:T(8,128)(2,1)}) %all-gather.11.cloned.1.call-update) | async-done | bytes 3932176 | tf_op jit(solution)/shard_map/all_gather | solution.py:221
  1297.2 509.4 %while.38 = (s32[]{:T(128)}, f32[2,1024,3,64]{1,3,2,0:T(8,128)}, f32[2,1024,3,64]{1,3,2,0:T(8,128)}, f32[3,2047]{1,0:T(4,128)}, bf16[2,2,512,3,64]{2,4,3,1,0:T(8...) while((s32[]{:T(128)}, f32[2,1024,3,64]{1,3,2,0:T(8,128)}, ...), condition=%wide.region_20.21_spmd.clone, body=%wide.region_16.20_spmd.clone.sunk | while | flops 2055205888 | bytes 419957216 | solution.py:274
  1307.1 21.8 %copy.85 = f32[1,3,513,1536]{3,1,2,0:T(4,128)S(1)} copy(f32[1,3,513,1536]{3,2,1,0:T(8,128)S(1)} %broadcast_bitcast_fusion.5) | data formatting | bytes 18911232 | tf_op jit(solution)/shard_map/while
  1347.6 16.6 reshape.299
  1370.7 48.5 %rev.33 = f32[3,512,1024]{2,1,0:T(8,128)} reverse(f32[3,512,1024]{2,1,0:T(8,128)} %slice.93), dimensions={1} | reverse | bytes 12582912 | tf_op jit(solution)/shard_map/while/body/eval_jaxpr/rev | solution.py:41
  1449.8 48.6 %rev.34 = f32[3,512,1024]{2,1,0:T(8,128)} reverse(f32[3,512,1024]{2,1,0:T(8,128)} %get-tuple-element.781), dimensions={1} | reverse | bytes 12582912 | tf_op jit(solution)/shard_map/while/body/eval_jaxpr/rev | solution.py:261
  1557.8 21.8 %copy.85 = f32[1,3,513,1536]{3,1,2,0:T(4,128)S(1)} copy(f32[1,3,513,1536]{3,2,1,0:T(8,128)S(1)} %broadcast_bitcast_fusion.5) | data formatting | bytes 18911232 | tf_op jit(solution)/shard_map/while
  1597.7 16.8 reshape.299
  1621.0 48.5 %rev.33 = f32[3,512,1024]{2,1,0:T(8,128)} reverse(f32[3,512,1024]{2,1,0:T(8,128)} %slice.93), dimensions={1} | reverse | bytes 12582912 | tf_op jit(solution)/shard_map/while/body/eval_jaxpr/rev | solution.py:41
  1699.8 48.6 %rev.34 = f32[3,512,1024]{2,1,0:T(8,128)} reverse(f32[3,512,1024]{2,1,0:T(8,128)} %get-tuple-element.781), dimensions={1} | reverse | bytes 12582912 | tf_op jit(solution)/shard_map/while/body/eval_jaxpr/rev | solution.py:261
  1841.4 101.5 %all-reduce.11.cloned.1.call-done = bf16[2048,768]{1,0:T(8,128)(2,1)} async-done(((bf16[2048,768]{1,0:T(8,128)(2,1)}), bf16[2048,768]{1,0:T(8,128)(2,1)}) %all-reduce.11.cloned.1.call-update) | async-done | bytes 3145744 | tf_op jit(solution)/shard_map/psum | solution.py:292
  1948.1 24.2 %all-reduce.5 = (f32[768]{0:T(1024)S(1)}, f32[32,3]{0,1:T(4,128)}, f32[768]{0:T(1024)S(1)}) all-reduce(f32[768]{0:T(1024)S(1)} %get-tuple-element.567, f32[32,3]{0,1:T(4,128)S(1)} %fusion.87, f32[768]{0:T(1024)S(1)} %copy-done.41), channel_id=4, replica_groups=mesh['dp'=4,'expert'=2,'tensor'=4] {'dp','expert'}, use_global_device_ids=true, to_apply=%region_24.25.clone | all-reduce | flops 1632 | bytes 13056
  1980.6 46.5 %reduce-scatter.14.cloned.1.call-done = f32[96,3,192]{2,0,1:T(8,128)} async-done(((f32[768,3,192]{2,0,1:T(8,128)}), f32[96,3,192]{2,0,1:T(8,128)}) %reduce-scatter.14.cloned.1.call-update) | async-done | bytes 221200 | tf_op jit(solution)/shard_map/reduce_scatter | solution.py:299
  (341 shorter events, 635.9 us)
Async XLA Ops:
  7.2 655.5 %copy-start = (bf16[1,768,768]{2,1,0:T(8,128)(2,1)S(1)}, bf16[1,768,768]{2,1,0:T(8,128)(2,1)}, u32[]{:S(2)}) copy-start(bf16[1,768,768]{2,1,0:T(8,128)(2,1)} %param.28) | copy-start | bytes 3538948
  7.2 540.0 %all-reduce.9.cloned.1.call-start = ((), (), s32[]{:S(2)}) async-start(), calls=%async_computation.11 | async-start | bytes 12582912 | tf_op jit(solution)/shard_map/psum | solution.py:118
  321.5 332.6 %all-gather.5.cloned.1.call-start = ((), (), s32[]{:S(2)}) async-start(), calls=%async_computation.12 | async-start | bytes 4915200 | tf_op jit(solution)/shard_map/all_gather | solution.py:164
  552.4 101.7 %copy-start.44 = (bf16[1,768,768]{2,1,0:T(8,128)(2,1)S(1)}, bf16[1,768,768]{2,1,0:T(8,128)(2,1)}, u32[]{:S(2)}) copy-start(bf16[1,768,768]{2,1,0:T(8,128)(2,1)} %param.27) | copy-start | bytes 3538948
  579.3 225.2 %reduce-scatter.10.cloned.1.call-start = ((), (), s32[]{:S(2)}) async-start(), calls=%async_computation.13 | async-start | bytes 9830400 | tf_op jit(solution)/shard_map/reduce_scatter | solution.py:171
  669.6 153.2 %copy-start.42 = (bf16[768,2]{0,1:T(2,128)(2,1)S(1)}, bf16[768,2]{0,1:T(2,128)(2,1)}, u32[]{:S(2)}) copy-start(bf16[768,2]{0,1:T(2,128)(2,1)} %param.26) | copy-start | bytes 9220
  669.6 229.3 %all-gather.7.cloned.1.call-start = ((), (), s32[]{:S(2)}) async-start(), calls=%async_computation.14 | async-start | bytes 4915200 | tf_op jit(solution)/shard_map/all_gather | solution.py:181
  822.7 191.9 %all-gather.9.cloned.1.call-start = ((), (), s32[]{:S(2)}) async-start(), calls=%async_computation.15 | async-start | bytes 4915200 | tf_op jit(solution)/shard_map/all_gather | solution.py:197
  940.3 228.2 %reduce-scatter.12.cloned.1.call-start = ((), (), s32[]{:S(2)}) async-start(), calls=%async_computation.16 | async-start | bytes 9830400 | tf_op jit(solution)/shard_map/reduce_scatter | solution.py:211
  1033.5 229.3 %all-gather.11.cloned.1.call-start = ((), (), s32[]{:S(2)}) async-start(), calls=%async_computation.17 | async-start | bytes 4915200 | tf_op jit(solution)/shard_map/all_gather | solution.py:221
  1186.6 649.2 %reduce-scatter.22.cloned.1.call-start = ((), (), s32[]{:S(2)}) async-start(), calls=%async_computation.23 | async-start | bytes 442368
  1192.7 644.5 %reduce-scatter.20.cloned.1.call-start = ((), (), s32[]{:S(2)}) async-start(), calls=%async_computation.22 | async-start | bytes 1474560 | tf_op jit(solution)/shard_map/reduce_scatter | solution.py:309
  1202.5 636.6 %reduce-scatter.18.cloned.1.call-start = ((), (), s32[]{:S(2)}) async-start(), calls=%async_computation.21 | async-start | bytes 1474560 | tf_op jit(solution)/shard_map/reduce_scatter | solution.py:306
  1202.5 72.5 %slice-start.3 = ((s8[6291456]{0:T(1024)(128)(4,1)}), s8[2097152]{0:T(1024)(128)(4,1)S(1)}, s32[]{:S(2)}) async-start(s8[6291456]{0:T(1024)(128)(4,1)} %bitcast.281), calls=%async_computation.27 | async-start | bytes 4194304
  1210.3 732.6 %all-reduce.11.cloned.1.call-start = ((), (), s32[]{:S(2)}) async-start(), calls=%async_computation.18 | async-start | bytes 6291456 | tf_op jit(solution)/shard_map/psum | solution.py:292
  1449.8 54.3 %copy-start.9 = (f32[2,1024,3,64]{1,3,2,0:T(8,128)S(1)}, f32[2,1024,3,64]{1,3,2,0:T(8,128)}, u32[]{:S(2)}) copy-start(f32[2,1024,3,64]{1,3,2,0:T(8,128)} %get-tuple-element.847) | copy-start | bytes 4718596 | tf_op jit(solution)/shard_map/while
  1699.8 54.4 %copy-start.9 = (f32[2,1024,3,64]{1,3,2,0:T(8,128)S(1)}, f32[2,1024,3,64]{1,3,2,0:T(8,128)}, u32[]{:S(2)}) copy-start(f32[2,1024,3,64]{1,3,2,0:T(8,128)} %get-tuple-element.847) | copy-start | bytes 4718596 | tf_op jit(solution)/shard_map/while
  1823.5 157.1 %reduce-scatter.16.cloned.1.call-start = ((), (), s32[]{:S(2)}) async-start(), calls=%async_computation.20 | async-start | bytes 884736 | tf_op jit(solution)/shard_map/reduce_scatter | solution.py:300
  1828.4 114.5 %copy-start.35 = (f32[2048]{0:T(1024)S(1)}, f32[2048]{0:T(1024)}, u32[]{:S(2)}) copy-start(f32[2048]{0:T(1024)} %copy-done.34) | copy-start | bytes 24580
  1828.4 114.5 %copy-start.40 = (f32[768]{0:T(1024)S(1)}, f32[768]{0:T(1024)}, u32[]{:S(2)}) copy-start(f32[768]{0:T(1024)} %copy-done.39) | copy-start | bytes 9220
  1828.5 198.6 %reduce-scatter.14.cloned.1.call-start = ((), (), s32[]{:S(2)}) async-start(), calls=%async_computation.19 | async-start | bytes 2654208 | tf_op jit(solution)/shard_map/reduce_scatter | solution.py:299
  1834.4 113.6 %copy-start.41 = (f32[768]{0:T(1024)S(1)}, f32[768]{0:T(1024)}, u32[]{:S(2)}) copy-start(f32[768]{0:T(1024)} %get-tuple-element.565) | copy-start | bytes 9220
  1834.4 139.0 %copy-start.38 = (f32[1,8,2,128]{3,2,1,0:T(2,128)S(1)}, f32[1,8,2,128]{3,2,1,0:T(2,128)}, u32[]{:S(2)}) copy-start(f32[1,8,2,128]{3,2,1,0:T(2,128)} %copy-done.37) | copy-start | bytes 24580
  1973.4 53.6 %copy-start.1 = (bf16[1,768,768]{2,1,0:T(8,128)(2,1)S(1)}, bf16[1,768,768]{2,1,0:T(8,128)(2,1)}, u32[]{:S(2)}) copy-start(bf16[1,768,768]{2,1,0:T(8,128)(2,1)} %param.28) | copy-start | bytes 3538948
  (64 other events, 454.1 us)
Sparse Core Ops, SparseCore 0:
  321.6 225.5 all-reduce.8
  579.5 74.5 all-gather.4
  669.7 134.8 reduce-scatter.9
  822.8 76.0 all-gather.6
  940.4 74.1 all-gather.8
  1033.6 134.8 reduce-scatter.11
  1186.7 76.0 all-gather.10
  1266.4 32.3 reduce-scatter.21
  1301.4 25.7 reduce-scatter.19
  1329.8 25.7 reduce-scatter.17
  1823.6 119.3 all-reduce.10
  1946.5 34.0 reduce-scatter.15
  1984.5 42.5 reduce-scatter.13
where the time goes:
time: 2060 us; the launch traced here: 2030 us
  waiting for transfers between devices  916 us (44%)
  local copies, waits for them, and re-layouts  683 us (33%)
  matrix products  212 us (10%)
  blocking collectives  89.9 us (4%)
  other arithmetic  84.8 us (4%)
  loops' own time  30.5 us (1%)
    psum x1, waiting for transfers between devices, per_device(): attn_total = lax.psum(attn_part, 'tensor')  224 us
    rev x4, local copies, waits for them, and re-layouts, bias_block(): return shifted[:, ::-1, :]  194 us
    while x74, local copies, waits for them, and re-layouts  181 us
    reduce_scatter x1, waiting for transfers between devices, per_device(): lax.psum_scatter(row_part, 'tensor', scatter_dimension=2, tiled=True)  135 us
    reduce_scatter x1, waiting for transfers between devices, per_device(): lax.psum_scatter(out_part, 'tensor', scatter_dimension=2, tiled=True)  135 us
    psum x1, waiting for transfers between devices, per_device(): lax.psum(d_in_part.astype(jnp.bfloat16), 'tensor').astype(jnp.float32)  102 us
    rev x2, local copies, waits for them, and re-layouts, backward_block(): head_sums = jnp.sum(d_scores.astype(jnp.float32), axis=0)[:, ::-1, :]  97.2 us
    all_gather x1, waiting for transfers between devices, per_device(): expert_in = lax.all_gather(part_in, 'tensor', axis=1, tiled=True)  74.3 us
  transfers between devices with their start and end apart: 13, of which 10 were waited for; matrix products, arithmetic and copies ran while one was open for 29% of the time, Pallas kernels for 0%

commit v1 on v0

v1 whole, which is shorter than its diff:
```python
import functools
import math

import jax
import jax.numpy as jnp
from jax import lax
from jax.experimental import pallas as pl
from jax.experimental.pallas import tpu as pltpu
from jax.sharding import PartitionSpec as P

HIGHEST_PRECISE = lax.Precision.HIGHEST
PAIR = 2
SUB = 128


def smooth(values_in):
    return (
        0.5
        * values_in
        * (
            1.0
            + jnp.tanh(
                0.7978845608028654 * (values_in + 0.044715 * values_in * values_in * values_in)
            )
        )
    )


def normed(values_in, gain_vec):
    return (
        values_in
        * lax.rsqrt(jnp.mean(values_in * values_in, axis=-1, keepdims=True) + 1e-06)
        * gain_vec
    )


def dot_nt(a, b):
    return lax.dot_general(a, b, (((1,), (1,)), ((), ())), preferred_element_type=jnp.float32)


def dot_nn(a, b):
    return jnp.dot(a, b, preferred_element_type=jnp.float32)


def build_bias(row, bias_buf):
    wide = jnp.broadcast_to(row, bias_buf.shape)
    bias_buf[...] = pltpu.roll(wide, 0, 1, stride=1, stride_axis=0)


def forward_kernel(hs, rows, q_ref, k_ref, v_ref, bias_ref, segq_ref, segk_ref, o_ref, lse_ref, bias_buf):
    length = k_ref.shape[0]
    scale = 1.0 / math.sqrt(hs)
    for h in range(PAIR):
        build_bias(bias_ref[h], bias_buf)
        cols = slice(h * hs, (h + 1) * hs)
        k_h = k_ref[:, cols]
        v_h = v_ref[:, cols]
        for b in range(rows // SUB):
            at = slice(b * SUB, (b + 1) * SUB)
            off = rows - b * SUB
            s = dot_nt(q_ref[at, cols], k_h) * scale + bias_buf[:, off : off + length]
            s = jnp.where(segq_ref[at, :] == segk_ref[...], s, -1e30)
            top = jnp.max(s, axis=-1, keepdims=True)
            e = jnp.exp(s - top)
            total = jnp.sum(e, axis=-1, keepdims=True)
            p = (e * (1.0 / total)).astype(jnp.bfloat16)
            o_ref[at, cols] = dot_nn(p, v_h).astype(jnp.bfloat16)
            lse_ref[h, at, :] = top + jnp.log(total)


def backward_kernel(
    hs, rows, q_ref, k_ref, v_ref, g_ref, bias_ref, segq_ref, segk_ref, lse_ref,
    dq_ref, dk_ref, dv_ref, drel_ref, bias_buf, drel_buf, p_buf, ds_buf,
):
    length = k_ref.shape[0]
    scale = 1.0 / math.sqrt(hs)
    width = bias_buf.shape[1]
    q_t = q_ref[...].T
    g_t = g_ref[...].T
    for h in range(PAIR):
        build_bias(bias_ref[h], bias_buf)
        drel_buf[...] = jnp.zeros_like(drel_buf)
        cols = slice(h * hs, (h + 1) * hs)
        k_h = k_ref[:, cols]
        v_h = v_ref[:, cols]
        for b in range(rows // SUB):
            at = slice(b * SUB, (b + 1) * SUB)
            off = rows - b * SUB
            s = dot_nt(q_ref[at, cols], k_h) * scale + bias_buf[:, off : off + length]
            s = jnp.where(segq_ref[at, :] == segk_ref[...], s, -1e30)
            p = jnp.exp(s - lse_ref[h, at, :])
            dp = dot_nt(g_ref[at, cols], v_h)
            ds = p * (dp - jnp.sum(p * dp, axis=-1, keepdims=True))
            ds = ds.astype(jnp.bfloat16)
            p_buf[at, :] = p.astype(jnp.bfloat16)
            ds_buf[at, :] = ds
            dq_ref[at, cols] = (dot_nn(ds, k_h) * scale).astype(jnp.bfloat16)
            drel_buf[:, off : off + length] += ds.astype(jnp.float32)
        dk_ref[cols, :] = dot_nn(q_t[cols, :], ds_buf[...]) * scale
        dv_ref[cols, :] = dot_nn(g_t[cols, :], p_buf[...])
        size = SUB
        while size > 8:
            size //= 2
            upper = pltpu.roll(drel_buf[size : 2 * size, :], width - size, 1)
            drel_buf[:size, :] += upper
        drel_ref[h] = drel_buf[:8, :]


def attend_forward(q, k, v, bias_rows, seg_q, seg_k, hs):
    rows, feats = q.shape
    length = k.shape[0]
    heads = feats // hs
    width = bias_rows.shape[2]
    lanes = PAIR * hs
    return pl.pallas_call(
        functools.partial(forward_kernel, hs, rows),
        grid=(heads // PAIR,),
        in_specs=[
            pl.BlockSpec((rows, lanes), lambda i: (0, i)),
            pl.BlockSpec((length, lanes), lambda i: (0, i)),
            pl.BlockSpec((length, lanes), lambda i: (0, i)),
            pl.BlockSpec((PAIR, 1, width), lambda i: (i, 0, 0)),
            pl.BlockSpec((rows, 1), lambda i: (0, 0)),
            pl.BlockSpec((1, length), lambda i: (0, 0)),
        ],
        out_specs=[
            pl.BlockSpec((rows, lanes), lambda i: (0, i)),
            pl.BlockSpec((PAIR, rows, 1), lambda i: (i, 0, 0)),
        ],
        out_shape=[
            jax.ShapeDtypeStruct((rows, feats), jnp.bfloat16),
            jax.ShapeDtypeStruct((heads, rows, 1), jnp.float32),
        ],
        scratch_shapes=[pltpu.VMEM((SUB, width), jnp.float32)],
        compiler_params=pltpu.CompilerParams(vmem_limit_bytes=40 * 1024 * 1024),
        cost_estimate=pl.CostEstimate(
            flops=4 * rows * length * feats, bytes_accessed=8 * length * feats,
            transcendentals=rows * length * heads,
        ),
        name="attend_forward",
    )(q, k, v, bias_rows, seg_q, seg_k)


def attend_backward(q, k, v, g, bias_rows, seg_q, seg_k, lse, hs):
    rows, feats = q.shape
    length = k.shape[0]
    heads = feats // hs
    width = bias_rows.shape[2]
    lanes = PAIR * hs
    return pl.pallas_call(
        functools.partial(backward_kernel, hs, rows),
        grid=(heads // PAIR,),
        in_specs=[
            pl.BlockSpec((rows, lanes), lambda i: (0, i)),
            pl.BlockSpec((length, lanes), lambda i: (0, i)),
            pl.BlockSpec((length, lanes), lambda i: (0, i)),
            pl.BlockSpec((rows, lanes), lambda i: (0, i)),
            pl.BlockSpec((PAIR, 1, width), lambda i: (i, 0, 0)),
            pl.BlockSpec((rows, 1), lambda i: (0, 0)),
            pl.BlockSpec((1, length), lambda i: (0, 0)),
            pl.BlockSpec((PAIR, rows, 1), lambda i: (i, 0, 0)),
        ],
        out_specs=[
            pl.BlockSpec((rows, lanes), lambda i: (0, i)),
            pl.BlockSpec((lanes, length), lambda i: (i, 0)),
            pl.BlockSpec((lanes, length), lambda i: (i, 0)),
            pl.BlockSpec((PAIR, 8, width), lambda i: (i, 0, 0)),
        ],
        out_shape=[
            jax.ShapeDtypeStruct((rows, feats), jnp.bfloat16),
            jax.ShapeDtypeStruct((feats, length), jnp.float32),
            jax.ShapeDtypeStruct((feats, length), jnp.float32),
            jax.ShapeDtypeStruct((heads, 8, width), jnp.float32),
        ],
        scratch_shapes=[
            pltpu.VMEM((SUB, width), jnp.float32),
            pltpu.VMEM((SUB, width), jnp.float32),
            pltpu.VMEM((rows, length), jnp.bfloat16),
            pltpu.VMEM((rows, length), jnp.bfloat16),
        ],
        compiler_params=pltpu.CompilerParams(vmem_limit_bytes=48 * 1024 * 1024),
        cost_estimate=pl.CostEstimate(
            flops=10 * rows * length * feats, bytes_accessed=20 * length * feats,
            transcendentals=rows * length * heads,
        ),
        name="attend_backward",
    )(q, k, v, g, bias_rows, seg_q, seg_k, lse)


def gather_rows(shard):
    copies = lax.axis_size("dp")
    part = shard.shape[0] // copies
    mine = lax.dynamic_slice_in_dim(shard, lax.axis_index("dp") * part, part, 0)
    return lax.all_gather(mine, ("tensor", "dp"), axis=0, tiled=True)


def per_device(
    tokens,
    segments,
    routes,
    rel_bucket,
    norm1_gain,
    query_key_value_weight,
    output_weight,
    bias_table,
    norm2_gain,
    w_router,
    w_in,
    w_expert_out,
    cotangent,
):
    seq_count, length, model_width = tokens.shape
    tok_count = seq_count * length
    heads_here = bias_table.shape[1]
    bucket_count = bias_table.shape[0]
    head_feat = query_key_value_weight.shape[2]
    hs = head_feat // heads_here
    experts = w_router.shape[1]
    local_exp = w_in.shape[0]
    ff_here = w_in.shape[2]
    peers = lax.axis_size("expert")
    splits = lax.axis_size("tensor")
    feats = head_feat * splits
    heads = heads_here * splits
    rank = lax.axis_index("tensor")
    capacity = tok_count * 5 // (4 * experts)
    share = tok_count // splits
    slots = min(capacity, share)
    per_seq = length // share
    seq_at = rank // per_seq
    seq_rank = rank % per_seq
    q_start = seq_rank * share
    own_start = rank * share

    def own(rows):
        return lax.dynamic_slice_in_dim(rows, own_start, share, 0)

    w_qkv_t = jnp.transpose(query_key_value_weight, (1, 2, 0)).reshape(3 * head_feat, model_width)
    table_rows = jnp.pad(bias_table.T, ((0, 64 - heads_here), (0, model_width - bucket_count)))
    qkv_all = gather_rows(jnp.concatenate([w_qkv_t, table_rows], 0))
    qkv_all = qkv_all.reshape(splits, 3 * head_feat + 64, model_width)
    table_all = qkv_all[:, 3 * head_feat : 3 * head_feat + heads_here, :bucket_count]
    table_all = table_all.reshape(heads, bucket_count).astype(jnp.float32)
    qkv_all = [
        qkv_all[:, c * head_feat : (c + 1) * head_feat].reshape(feats, model_width)
        for c in range(3)
    ]
    w_out_all = lax.all_gather(output_weight.T, "tensor", axis=0, tiled=True)
    w_in_all = gather_rows(w_in.reshape(local_exp * model_width, ff_here).T)
    w_eout_all = gather_rows(w_expert_out.reshape(local_exp * model_width, ff_here).T)

    gain_one = norm1_gain.astype(jnp.float32)
    gain_two = norm2_gain.astype(jnp.float32)
    seq_tokens = lax.dynamic_index_in_dim(tokens, seq_at, 0, keepdims=False).astype(jnp.float32)
    seq_seg = lax.dynamic_index_in_dim(segments, seq_at, 0, keepdims=False)
    a_in = normed(seq_tokens, gain_one).astype(jnp.bfloat16)
    x_own = lax.dynamic_slice_in_dim(seq_tokens, q_start, share, 0)
    a_own = lax.dynamic_slice_in_dim(a_in, q_start, share, 0)
    seg_q = lax.dynamic_slice_in_dim(seq_seg, q_start, share, 0)[:, None]
    seg_k = seq_seg[None, :]

    padded = jnp.pad(rel_bucket, (0, 1), constant_values=bucket_count)
    roll_start = lax.rem(3 * length - 1 - share - q_start, 2 * length)
    rolled = lax.dynamic_slice_in_dim(
        jnp.concatenate([padded, padded]), roll_start, 2 * length, 0
    )
    bucket_hot = (rolled[None, :] == jnp.arange(bucket_count, dtype=jnp.int32)[:, None]).astype(
        jnp.float32
    )
    bias_rows = jnp.dot(table_all, bucket_hot, precision=HIGHEST_PRECISE)[:, None, :]

    def project(rows, weight):
        return jnp.einsum(
            "td,fd->tf", rows, weight, preferred_element_type=jnp.float32
        ).astype(jnp.bfloat16)

    queries = project(a_own, qkv_all[0])
    keys = project(a_in, qkv_all[1])
    values = project(a_in, qkv_all[2])
    mixed, lse = attend_forward(queries, keys, values, bias_rows, seg_q, seg_k, hs)
    attn = jnp.einsum("tf,fd->td", mixed, w_out_all, preferred_element_type=jnp.float32)
    residual = x_own + attn
    moe_in = normed(residual, gain_two).astype(jnp.bfloat16)
    router_f = w_router.astype(jnp.float32)
    route_own = own(routes.reshape(tok_count))
    chosen = (route_own[:, None] == jnp.arange(experts, dtype=jnp.int32)[None, :]).astype(
        jnp.float32
    )

    def gate_of(rows_in, router_in):
        logits = jnp.dot(rows_in, router_in, precision=HIGHEST_PRECISE)
        return jnp.sum(jax.nn.softmax(logits, axis=-1) * chosen, axis=-1)

    gate_value, gate_back = jax.vjp(gate_of, moe_in.astype(jnp.float32), router_f)
    grad_output = own(cotangent.reshape(tok_count, model_width)).astype(jnp.float32)
    d_rows_tok = (gate_value[:, None] * grad_output).astype(jnp.bfloat16)

    direct = slots == share and peers == 2 and experts == 2
    here = lax.axis_index("expert")
    swap = [(0, 1), (1, 0)]
    if direct:
        at_self = (route_own == here)[:, None]

        def to_slots(rows_tok):
            none = jnp.zeros_like(rows_tok)
            return (jnp.where(at_self, rows_tok, none), jnp.where(at_self, none, rows_tok))

        def from_slots(rows_slot):
            return jnp.where(at_self, rows_slot[0], rows_slot[1]).astype(jnp.float32)

    elif slots == share:
        chosen_b = chosen.astype(jnp.bfloat16)

        def to_slots(rows_tok):
            return jnp.stack([rows_tok * chosen_b[:, e : e + 1] for e in range(experts)])

        def from_slots(rows_slot):
            total = rows_slot[0].astype(jnp.float32) * chosen[:, 0:1]
            for e in range(1, experts):
                total = total + rows_slot[e].astype(jnp.float32) * chosen[:, e : e + 1]
            return total

    else:
        tok_pos = jnp.arange(share, dtype=jnp.int32)
        earlier = (tok_pos[:, None] > tok_pos[None, :]).astype(jnp.bfloat16)
        before = jnp.dot(earlier, chosen.astype(jnp.bfloat16), preferred_element_type=jnp.float32)
        slot_rank = jnp.sum(before * chosen, axis=1).astype(jnp.int32)
        place = route_own * slots + slot_rank
        place_hot = (
            place[:, None] == jnp.arange(experts * slots, dtype=jnp.int32)[None, :]
        ).astype(jnp.bfloat16)

        def to_slots(rows_tok):
            return (
                jnp.einsum("tp,td->pd", place_hot, rows_tok, preferred_element_type=jnp.float32)
                .astype(jnp.bfloat16)
                .reshape(experts, slots, model_width)
            )

        def from_slots(rows_slot):
            return jnp.einsum(
                "tp,pd->td",
                place_hot,
                rows_slot.reshape(experts * slots, model_width),
                preferred_element_type=jnp.float32,
            )

    def exchange(rows):
        if direct:
            return jnp.stack([rows[0], lax.ppermute(rows[1], "expert", swap)])
        return lax.all_to_all(rows, "expert", split_axis=0, concat_axis=0, tiled=True)

    sent_rows = exchange(to_slots(moe_in))
    sent_grad = exchange(to_slots(d_rows_tok))
    slot_total = peers * slots
    w_in_e = w_in_all.reshape(splits * ff_here, local_exp, model_width)
    w_eout_e = w_eout_all.reshape(splits * ff_here, local_exp, model_width)
    expert_in = sent_rows.reshape(peers, local_exp, slots, model_width)
    grad_rows = sent_grad.reshape(peers, local_exp, slots, model_width)

    def narrow_dot(left, right):
        return jnp.einsum("cf,fd->cd", left, right, preferred_element_type=jnp.float32).astype(
            jnp.bfloat16
        )

    def back_rows(left, right):
        if direct:
            away = lax.ppermute(narrow_dot(left[slots:], right), "expert", swap)
            return (narrow_dot(left[:slots], right), away)
        return narrow_dot(left, right).reshape(peers, 1, slots, model_width)

    out_list, row_list, gin_list, gout_list = [], [], [], []
    for e in range(local_exp):
        wi = w_in_e[:, e]
        wo = w_eout_e[:, e]
        rows_e = expert_in[:, e].reshape(slot_total, model_width)
        grad_e = grad_rows[:, e].reshape(slot_total, model_width)
        hidden = jnp.einsum("cd,fd->cf", rows_e, wi, preferred_element_type=jnp.float32)
        active = smooth(hidden).astype(jnp.bfloat16)
        out_list.append(back_rows(active, wo))
        d_active = jnp.einsum("cd,fd->cf", grad_e, wo, preferred_element_type=jnp.float32)
        d_hidden = jax.vjp(smooth, hidden)[1](d_active)[0].astype(jnp.bfloat16)
        row_list.append(back_rows(d_hidden, wi))
        gout_list.append(
            jnp.einsum("cd,cf->df", grad_e, active, preferred_element_type=jnp.float32).astype(
                jnp.bfloat16
            )
        )
        gin_list.append(
            jnp.einsum("cd,cf->df", rows_e, d_hidden, preferred_element_type=jnp.float32).astype(
                jnp.bfloat16
            )
        )

    def home(parts):
        if direct:
            return parts[0]
        return exchange(jnp.concatenate(parts, 1).reshape(experts, slots, model_width))

    returned = home(out_list)
    row_back = home(row_list)
    expert_rows = from_slots(returned)
    output_own = (residual + gate_value[:, None] * expert_rows).astype(jnp.bfloat16)
    output = lax.all_gather(output_own, "tensor", axis=0, tiled=True).reshape(tokens.shape)
    d_gate = jnp.sum(grad_output * expert_rows, axis=-1)
    d_router_in, d_router = gate_back(d_gate)
    d_moe = from_slots(row_back) + d_router_in
    d_resid_norm, d_gain_two = jax.vjp(normed, residual, gain_two)[1](d_moe)
    d_residual = grad_output + d_resid_norm
    d_attn_out = d_residual.astype(jnp.bfloat16)
    d_mixed = jnp.einsum(
        "td,fd->tf", d_attn_out, w_out_all, preferred_element_type=jnp.float32
    ).astype(jnp.bfloat16)

    grad_w_out = jnp.einsum("td,tf->df", d_attn_out, mixed, preferred_element_type=jnp.float32)
    groups = ("dp", "expert")
    group_count = lax.axis_size("dp") * peers
    part = model_width // group_count

    def by_shard(grad, columns):
        sent = grad.astype(jnp.bfloat16).reshape(group_count, part, columns, splits, head_feat)
        sent = jnp.transpose(sent, (0, 3, 1, 2, 4))
        return sent.reshape(group_count, splits, part, columns * head_feat)

    def dense_total(sent):
        sent = sent.reshape(group_count * splits * part, -1)
        over = lax.psum_scatter(sent, groups, scatter_dimension=0, tiled=True)
        over = lax.psum_scatter(over, "tensor", scatter_dimension=0, tiled=True)
        return over.astype(jnp.float32)

    def over_dp(grads):
        per = grads[0][None] if local_exp == 1 else jnp.stack(grads, 0)
        return lax.psum_scatter(per, "dp", scatter_dimension=1, tiled=True)

    def over_tensor(summed):
        summed = summed.reshape(local_exp, summed.shape[1], splits, ff_here)
        summed = jnp.transpose(summed, (2, 0, 1, 3))
        summed = lax.psum_scatter(summed, "tensor", scatter_dimension=0, tiled=True)
        return summed[0].astype(jnp.float32)

    out_sent = by_shard(grad_w_out, 1)
    d_mixed, out_sent, gout_list, gin_list, output = lax.optimization_barrier(
        (d_mixed, out_sent, gout_list, gin_list, output)
    )
    gout_dp = over_dp(gout_list)
    gin_dp = over_dp(gin_list)
    out_total = dense_total(out_sent)

    d_queries, dk_t, dv_t, d_rel = attend_backward(
        queries, keys, values, d_mixed, bias_rows, seg_q, seg_k, lse, hs
    )
    dk_t, dv_t, d_queries, gout_dp = lax.optimization_barrier((dk_t, dv_t, d_queries, gout_dp))

    def key_part(index):
        at = index * share
        return (
            lax.dynamic_slice_in_dim(dk_t, at, share, 1),
            lax.dynamic_slice_in_dim(dv_t, at, share, 1),
        )

    mine = key_part(seq_rank)
    for step in range(1, per_seq):
        sends = [
            (r, r // per_seq * per_seq + (r % per_seq + step) % per_seq) for r in range(splits)
        ]
        piece = key_part((seq_rank + step) % per_seq)
        piece = jnp.concatenate([half.astype(jnp.bfloat16) for half in piece], 0)
        piece = lax.ppermute(piece, "tensor", sends).astype(jnp.float32)
        mine = (mine[0] + piece[:feats], mine[1] + piece[feats:])
    dkv_own = [half.astype(jnp.bfloat16) for half in mine]
    dkv_own, gin_dp = lax.optimization_barrier((dkv_own, gin_dp))
    grad_eout_total = over_tensor(gout_dp)
    grad_in_total = over_tensor(gin_dp)
    grad_q = jnp.einsum("td,tf->df", a_own, d_queries, preferred_element_type=jnp.float32)
    grad_k = jnp.einsum("td,ft->df", a_own, dkv_own[0], preferred_element_type=jnp.float32)
    grad_v = jnp.einsum("td,ft->df", a_own, dkv_own[1], preferred_element_type=jnp.float32)
    d_in_total = (
        jnp.einsum("tf,fd->td", d_queries, qkv_all[0], preferred_element_type=jnp.float32)
        + jnp.einsum("ft,fd->td", dkv_own[0], qkv_all[1], preferred_element_type=jnp.float32)
        + jnp.einsum("ft,fd->td", dkv_own[1], qkv_all[2], preferred_element_type=jnp.float32)
    )
    d_inputs, d_gain_one = jax.vjp(normed, x_own, gain_one)[1](d_in_total)
    grad_own = (d_inputs + d_residual).astype(jnp.bfloat16)
    input_grad = lax.all_gather(grad_own, "tensor", axis=0, tiled=True).reshape(tokens.shape)

    width = 2 * length
    unskewed = d_rel[:, 0]
    for a in range(1, 8):
        unskewed = unskewed + jnp.pad(d_rel[:, a, a:], ((0, 0), (0, a)))
    grad_table_all = lax.dot_general(
        bucket_hot, unskewed, (((1,), (1,)), ((), ())), precision=HIGHEST_PRECISE
    )

    table_cols = -(-bucket_count * heads_here // part)
    table_sent = jnp.transpose(grad_table_all.reshape(bucket_count, splits, heads_here), (1, 0, 2))
    table_sent = table_sent.reshape(splits, bucket_count * heads_here)
    table_sent = jnp.pad(table_sent, ((0, 0), (0, table_cols * part - bucket_count * heads_here)))
    table_sent = table_sent.reshape(1, splits, part, table_cols)
    gain_sent = jnp.concatenate([d_gain_one[:, None], d_gain_two[:, None], d_router], 1)
    gain_cols = 2 + experts
    gain_sent = gain_sent.reshape(group_count, 1, part, gain_cols)
    sent = jnp.concatenate(
        [by_shard(grad, 1) for grad in (grad_q, grad_k, grad_v)]
        + [
            jnp.broadcast_to(gain_sent, (group_count, splits, part, gain_cols)).astype(
                jnp.bfloat16
            ),
            jnp.broadcast_to(table_sent, (group_count, splits, part, table_cols)).astype(
                jnp.bfloat16
            ),
        ],
        -1,
    )
    sums = dense_total(sent)
    qkv_cols = 3 * head_feat
    qkv_total = sums[:, :qkv_cols].reshape(part, 3, head_feat)
    gains = sums[:, qkv_cols : qkv_cols + gain_cols]
    table_total = sums[:, qkv_cols + gain_cols :].reshape(-1)[: bucket_count * heads_here]
    return (
        output,
        input_grad,
        gains[:, 0],
        qkv_total,
        out_total,
        table_total.reshape(bucket_count, heads_here),
        gains[:, 1],
        gains[:, 2:],
        grad_in_total,
        grad_eout_total,
    )


def solution(mesh):
    placed = (
        P(("dp", "expert"), None, None),
        P(("dp", "expert"), None),
        P(("dp", "expert"), None, None),
        P(),
        P(),
        P(None, None, "tensor"),
        P(None, "tensor"),
        P(None, "tensor"),
        P(),
        P(),
        P("expert", None, "tensor"),
        P("expert", None, "tensor"),
        P(("dp", "expert"), None, None),
    )
    return jax.shard_map(
        per_device,
        mesh=mesh,
        in_specs=placed,
        out_specs=(
            P(("dp", "expert"), None, None),
            P(("dp", "expert"), None, None),
            P(("dp", "expert")),
            P(("dp", "expert"), None, "tensor"),
            P(("dp", "expert"), "tensor"),
            P(None, "tensor"),
            P(("dp", "expert")),
            P(("dp", "expert"), None),
            P("expert", "dp", "tensor"),
            P("expert", "dp", "tensor"),
        ),
        check_vma=False,
    )
```

time: 2060 us -> 765 us (0.37)
  local copies, waits for them, and re-layouts: 683 us -> 110 us
  waiting for transfers between devices: 916 us -> 449 us
  matrix products: 212 us -> 94.6 us
  blocking collectives: 89.9 us -> 0 us
  other arithmetic: 84.8 us -> 25.7 us
  Pallas kernels: 0 us -> 56.1 us
  loops' own time: 30.5 us -> 0 us
    psum x2 -> x0, waiting for transfers between devices: 326 us -> none  [the longest x1 224 us: per_device(): attn_total = lax.psum(attn_part, 'tensor')]
    rev x6 -> x0, local copies, waits for them, and re-layouts: 291 us -> none  [the longest x4 194 us: bias_block(): return shifted[:, ::-1, :]]
    reduce_scatter x6, waiting for transfers between devices: 317 us -> 95.9 us  [the longest x2 57 us: over_tensor(): summed = lax.psum_scatter(summed, 'tensor', scatter_dimension=0, tiled=True)]
    while x77 -> x0, local copies, waits for them, and re-layouts: 187 us -> none
    dot_general x32 -> x22, matrix products: 195 us -> 93 us  [the longest x1 17.1 us: per_device(): jnp.einsum('cd,fd->cf', grad_e, wo, preferred_element_type=jnp.float32)]
    ppermute x0 -> x5, waiting for transfers between devices: none -> 85.3 us  [the longest x2 35.7 us: exchange(): return jnp.stack([rows[0], lax.ppermute(rows[1], 'expert', swap)])]
    reshape x8 -> x7, local copies, waits for them, and re-layouts: 97.5 us -> 22 us  [the longest x4 17.1 us: by_shard(): grad.astype(jnp.bfloat16)]
    all_gather x4 -> x6, waiting for transfers between devices: 274 us -> 203 us  [the longest x3 107 us: gather_rows(): return lax.all_gather(mine, ('tensor', 'dp'), axis=0, tiled=True)]
  transfers between devices with their start and end apart: 13 -> 19, of which waited for: 10 -> 17; matrix products, arithmetic and copies ran while one was open for 29% -> 22% of each run, Pallas kernels for 0% -> 7%
where the time goes in v1:
time: 765 us; the launch traced here: 759 us
  waiting for transfers between devices  449 us (59%)
  local copies, waits for them, and re-layouts  110 us (14%)
  matrix products  94.6 us (12%)
  Pallas kernels  56.1 us (7%)
  other arithmetic  25.7 us (3%)
  between operations  15 us (2%)
  starting transfers between devices  8.19 us (1%)
    all_gather x3, waiting for transfers between devices, gather_rows(): return lax.all_gather(mine, ('tensor', 'dp'), axis=0, tiled=True)  107 us
    unnamed x16, waiting for transfers between devices  65.4 us
    all_gather x1, waiting for transfers between devices, per_device(): lax.all_gather(grad_own, 'tensor', axis=0, tiled=True).reshape(tokens.shape)  62 us
    reduce_scatter x2, waiting for transfers between devices, over_tensor(): summed = lax.psum_scatter(summed, 'tensor', scatter_dimension=0, tiled=True)  57 us
    ppermute x2, waiting for transfers between devices, exchange(): return jnp.stack([rows[0], lax.ppermute(rows[1], 'expert', swap)])  35.7 us
    all_gather x1, waiting for transfers between devices, per_device(): lax.all_gather(output_own, 'tensor', axis=0, tiled=True)  34.1 us
    ppermute x2, waiting for transfers between devices, back_rows(): away = lax.ppermute(narrow_dot(left[slots:], right), 'expert', swap)  33.5 us
    pallas_call x1, Pallas kernels, attend_backward(): pl.pallas_call(functools.partial(backward_kernel, hs, rows), grid=(heads...  31.4 us
  transfers between devices with their start and end apart: 19, of which 17 were waited for; matrix products, arithmetic and copies ran while one was open for 22% of the time, Pallas kernels for 7%

profile of v1, /device:TPU:0, one launch (start us, length us, event | category | flops | bytes accessed | tf_op | source)
XLA Modules:
  0.0 758.8 jit_solution(14353217881644170722)
XLA Ops:
  21.1 41.3 %all-gather.7.cloned.1.call-done = bf16[2560,768]{1,0:T(8,128)(2,1)} async-done(((bf16[160,768]{1,0:T(8,128)(2,1)}), bf16[2560,768]{1,0:T(8,128)(2,1)}) %all-gather.7.cloned.1.call-update) | async-done | bytes 3932176 | tf_op jit(solution)/shard_map/all_gather | solution.py:194
  71.7 24.7 %attend_forward.1 = (bf16[512,768]{1,0:T(8,128)(2,1)S(1)}, f32[12,512,1]{2,1,0:T(8,128)S(1)}) custom-call(bf16[512,768]{1,0:T(8,128)(2,1)S(1)} %convolution_convert_fusion.9.q_ref, bf16[1024,768]{1,0:T(8,128)(2,1)S(1)} %convolution_convert_fusion.3.k_ref, bf16[1024,768]{1,0:T(8,128)(2,1)S(1)} %convolution_convert_fusion.2.v_ref, ...), custom_call_target="tpu_custom_call" | custom-call | flops 1610612736 | bytes 6291456 | tf_op jit(solution)/shard_map/attend_forward/pallas_call | solution.py:115
  105.2 18.2 %collective-permute-done = bf16[512,768]{1,0:T(8,128)(2,1)S(1)} collective-permute-done((bf16[512,768]{1,0:T(8,128)(2,1)S(1)}, bf16[512,768]{1,0:T(8,128)(2,1)S(1)}, u32[]{:S(2)}, u32[]{:S(2)}) %collective-permute-start) | collective-permute-done | bytes 786464 | tf_op jit(solution)/shard_map/ppermute | solution.py:350
  124.8 23.6 %all-gather.11.cloned.1.call-done = bf16[3072,768]{1,0:T(8,128)(2,1)} async-done(((bf16[192,768]{1,0:T(8,128)(2,1)}), bf16[3072,768]{1,0:T(8,128)(2,1)}) %all-gather.11.cloned.1.call-update) | async-done | bytes 4718608 | tf_op jit(solution)/shard_map/all_gather | solution.py:194
  148.4 12.9 %multiply_convert_fusion = (bf16[1024,3072]{1,0:T(8,128)(2,1)}, f32[1024,3072]{1,0:T(8,128)}) fusion(bf16[1024,768]{1,0:T(8,128)(2,1)} %bitcast.188, bf16[3072,768]{1,0:T(8,128)(2,1)} %all-gather.11.cloned.1.call-done), kind=kOutput, calls=%fused_computation.10 | convolution fusion | flops 4860149760 | bytes 25165824 | tf_op jit(solution)/shard_map/cd,fd->cf/dot_general | solution.py:378
  161.3 41.8 %all-gather.13.cloned.1.call-done = bf16[3072,768]{1,0:T(8,128)(2,1)} async-done(((bf16[192,768]{1,0:T(8,128)(2,1)}), bf16[3072,768]{1,0:T(8,128)(2,1)}) %all-gather.13.cloned.1.call-update) | async-done | bytes 4718608 | tf_op jit(solution)/shard_map/all_gather | solution.py:194
  211.0 17.9 %collective-permute-done.3 = bf16[512,768]{1,0:T(8,128)(2,1)S(1)} collective-permute-done((bf16[512,768]{1,0:T(8,128)(2,1)S(1)}, bf16[512,768]{1,0:T(8,128)(2,1)S(1)}, u32[]{:S(2)}, u32[]{:S(2)}) %collective-permute-start.3) | collective-permute-done | bytes 786464 | tf_op jit(solution)/shard_map/ppermute | solution.py:368
  233.6 17.4 %collective-permute-done.1 = bf16[512,768]{1,0:T(8,128)(2,1)S(1)} collective-permute-done((bf16[512,768]{1,0:T(8,128)(2,1)S(1)}, bf16[512,768]{1,0:T(8,128)(2,1)S(1)}, u32[]{:S(2)}, u32[]{:S(2)}) %collective-permute-start.1) | collective-permute-done | bytes 786464 | tf_op jit(solution)/shard_map/ppermute | solution.py:350
  251.2 17.1 %fusion.3 = bf16[1024,3072]{1,0:T(8,128)(2,1)S(1)} fusion(f32[1024,3072]{1,0:T(8,128)} %get-tuple-element.103, bf16[1024,768]{1,0:T(8,128)(2,1)S(1)} %bitcast.190, bf16[3072,768]{1,0:T(8,128)(2,1)S(1)} %copy-done.42), kind=kOutput, calls=%fused_computation.7 | convolution fusion | flops 4907335680 | bytes 25165824 | tf_op jit(solution)/shard_map/cd,fd->cf/dot_general | solution.py:381
  273.4 15.6 %collective-permute-done.2 = bf16[512,768]{1,0:T(8,128)(2,1)S(1)} collective-permute-done((bf16[512,768]{1,0:T(8,128)(2,1)S(1)}, bf16[512,768]{1,0:T(8,128)(2,1)S(1)}, u32[]{:S(2)}, u32[]{:S(2)}) %collective-permute-start.2) | collective-permute-done | bytes 786464 | tf_op jit(solution)/shard_map/ppermute | solution.py:368
  295.7 10.1 %convolution_convert_fusion = bf16[768,3072]{1,0:T(8,128)(2,1)} fusion(bf16[1024,768]{1,0:T(8,128)(2,1)} %bitcast.189, bf16[1024,3072]{1,0:T(8,128)(2,1)} %copy-done.43), kind=kOutput, calls=%fused_computation.11 | convolution fusion | flops 4834197504 | bytes 12582912 | tf_op jit(solution)/shard_map/cd,cf->df/dot_general | solution.py:390
  305.8 9.6 %convolution_convert_fusion.1 = bf16[768,3072]{1,0:T(8,128)(2,1)} fusion(bf16[1024,768]{1,0:T(8,128)(2,1)S(1)} %bitcast.191, bf16[1024,3072]{1,0:T(8,128)(2,1)} %get-tuple-element.102), kind=kOutput, calls=%fused_computation.12 | convolution fusion | flops 4834197504 | bytes 12582912 | tf_op jit(solution)/shard_map/cd,cf->df/dot_general | solution.py:385
  323.8 34.1 %all-gather.15.cloned.1.call-done = bf16[2048,768]{1,0:T(8,128)(2,1)} async-done(((bf16[512,768]{1,0:T(8,128)(2,1)}), bf16[2048,768]{1,0:T(8,128)(2,1)}) %all-gather.15.cloned.1.call-update) | async-done | bytes 3145744 | tf_op jit(solution)/shard_map/all_gather | solution.py:404
  361.3 31.4 %attend_backward.1 = (bf16[512,768]{1,0:T(8,128)(2,1)S(1)}, f32[768,1024]{1,0:T(8,128)}, f32[768,1024]{1,0:T(8,128)}, f32[12,8,2048]{2,1,0:T(8,128)S(1)}) custom-call(bf16[512,768]{1,0:T(8,128)(2,1)S(1)} %convolution_convert_fusion.9.q_ref, bf16[1024,768]{1,0:T(8,128)(2,1)S(1)} %copy-done.4, bf16[1024,768]{1,0:T(8,128)(2,1)} %copy-done.2, ...), custom_call_target="tpu_custom_call" | custom-call | flops 4026531840 | bytes 15728640 | tf_op jit(solution)/shard_map/attend_backward/pallas_call | solution.py:150
  394.2 12.5 %reduce-scatter.13.cloned.1.call-done = bf16[1,192,3072]{2,1,0:T(8,128)(2,1)} async-done(((bf16[1,768,3072]{2,1,0:T(8,128)(2,1)}), bf16[1,192,3072]{2,1,0:T(8,128)(2,1)}) %reduce-scatter.13.cloned.1.call-update) | async-done | bytes 1179664 | tf_op jit(solution)/shard_map/reduce_scatter | solution.py:433
  431.3 16.1 %collective-permute-done.4 = bf16[1536,512]{1,0:T(8,128)(2,1)} collective-permute-done((bf16[1536,512]{1,0:T(8,128)(2,1)}, bf16[1536,512]{1,0:T(8,128)(2,1)}, u32[]{:S(2)}, u32[]{:S(2)}) %collective-permute-start.4) | collective-permute-done | bytes 1572896 | tf_op jit(solution)/shard_map/ppermute | solution.py:468
  497.9 18.0 %concatenate.43 = bf16[3072,581]{0,1:T(8,128)(2,1)} concatenate(bf16[3072,192]{0,1:T(8,128)(2,1)} %concatenate.35, bf16[3072,192]{0,1:T(8,128)(2,1)} %concatenate.36, bf16[3072,192]{0,1:T(8,128)(2,1)} %concatenate.37, bf16[3072,4]{0,1:T(4,128)(2,1)S(1)} %concatenate.42, bf16[3072,1]{0,1:T(2,128)(2,1)S(1)} %broadcast_in_dim.94), dimensions={1} | concatenate | bytes 7139328 | tf_op jit(solution)/shard_map/concatenate | solution.py:502
  516.0 6.1 copy.75
  531.1 41.3 %reduce-scatter.25.cloned.1.call-done = bf16[384,581]{1,0:T(8,128)(2,1)} async-done(((bf16[3072,581]{1,0:T(8,128)(2,1)}), bf16[384,581]{1,0:T(8,128)(2,1)}) %reduce-scatter.25.cloned.1.call-update) | async-done | bytes 446224
  572.5 21.5 %reduce-scatter.19.cloned.1.call-done = bf16[96,192]{1,0:T(8,128)(2,1)} async-done(((bf16[384,192]{1,0:T(8,128)(2,1)}), bf16[96,192]{1,0:T(8,128)(2,1)}) %reduce-scatter.19.cloned.1.call-update) | async-done | bytes 36880 | tf_op jit(solution)/shard_map/reduce_scatter | solution.py:428
  595.4 28.3 %reduce-scatter.23.cloned.1.call-done = bf16[1,1,192,768]{3,2,1,0:T(8,128)(2,1)} async-done(((bf16[4,1,192,768]{3,2,1,0:T(8,128)(2,1)}), bf16[1,1,192,768]{3,2,1,0:T(8,128)(2,1)}) %reduce-scatter.23.cloned.1.call-update) | async-done | bytes 294928 | tf_op jit(solution)/shard_map/reduce_scatter | solution.py:438
  625.7 28.7 %reduce-scatter.21.cloned.1.call-done = bf16[1,1,192,768]{3,2,1,0:T(8,128)(2,1)} async-done(((bf16[4,1,192,768]{3,2,1,0:T(8,128)(2,1)}), bf16[1,1,192,768]{3,2,1,0:T(8,128)(2,1)}) %reduce-scatter.21.cloned.1.call-update) | async-done | bytes 294928 | tf_op jit(solution)/shard_map/reduce_scatter | solution.py:438
  656.2 62.0 %all-gather.17.cloned.1.call-done = bf16[2048,768]{1,0:T(8,128)(2,1)} async-done(((bf16[512,768]{1,0:T(8,128)(2,1)}), bf16[2048,768]{1,0:T(8,128)(2,1)}) %all-gather.17.cloned.1.call-update) | async-done | bytes 3145744 | tf_op jit(solution)/shard_map/all_gather | solution.py:484
  718.2 22.1 %reduce-scatter.27.cloned.1.call-done = bf16[96,581]{1,0:T(8,128)(2,1)} async-done(((bf16[384,581]{1,0:T(8,128)(2,1)}), bf16[96,581]{1,0:T(8,128)(2,1)}) %reduce-scatter.27.cloned.1.call-update) | async-done | bytes 111568
  (239 shorter events, 171.4 us)
Async XLA Ops:
  7.2 55.2 %all-gather.7.cloned.1.call-start = ((), (), s32[]{:S(2)}) async-start(), calls=%async_computation.8 | async-start | bytes 4177920 | tf_op jit(solution)/shard_map/all_gather | solution.py:194
  9.0 90.3 %all-gather.9.cloned.1.call-start = ((), (), s32[]{:S(2)}) async-start(), calls=%async_computation.9 | async-start | bytes 1474560 | tf_op jit(solution)/shard_map/all_gather | solution.py:248
  9.8 138.6 %all-gather.11.cloned.1.call-start = ((), (), s32[]{:S(2)}) async-start(), calls=%async_computation.10 | async-start | bytes 5013504 | tf_op jit(solution)/shard_map/all_gather | solution.py:194
  14.3 188.7 %all-gather.13.cloned.1.call-start = ((), (), s32[]{:S(2)}) async-start(), calls=%async_computation.11 | async-start | bytes 5013504 | tf_op jit(solution)/shard_map/all_gather | solution.py:194
  16.3 341.5 %all-gather.15.cloned.1.call-start = ((), (), s32[]{:S(2)}) async-start(), calls=%async_computation.12 | async-start | bytes 3932160 | tf_op jit(solution)/shard_map/all_gather | solution.py:404
  17.9 213.8 %copy-start.36 = (pred[512]{0:T(512)(128)(4,1)}, pred[512]{0:T(512)(128)(4,1)S(1)}, u32[]{:S(2)}) copy-start(pred[512]{0:T(512)(128)(4,1)S(1)} %get-tuple-element.84) | copy-start | bytes 1540
  21.1 44.5 %copy-start.29 = (bf16[512,768]{1,0:T(8,128)(2,1)}, bf16[512,768]{1,0:T(8,128)(2,1)S(1)}, u32[]{:S(2)}) copy-start(bf16[512,768]{1,0:T(8,128)(2,1)S(1)} %get-tuple-element.110) | copy-start | bytes 2359300
  101.9 187.1 %copy-start.9 = (f32[512,768]{1,0:T(8,128)}, f32[512,768]{1,0:T(8,128)S(1)}, u32[]{:S(2)}) copy-start(f32[512,768]{1,0:T(8,128)S(1)} %get-tuple-element.101) | copy-start | bytes 4718596
  103.7 19.8 %collective-permute-start = (bf16[512,768]{1,0:T(8,128)(2,1)S(1)}, bf16[512,768]{1,0:T(8,128)(2,1)S(1)}, u32[]{:S(2)}, u32[]{:S(2)}) collective-permute-start(bf16[512,768]{1,0:T(8,128)(2,1)S(1)} %broadcast_select_fusion.1), channel_id=1, source_target_pairs={{0,4},{4,0},{1,5},{5,1},{2,6},{6,2},{3,7},{7,3},{8,12},{12,8},{9,1... | collective-permute-start | bytes 2359304 | tf_op jit(solution)/shard_map/ppermute | solution.py:350
  209.1 19.8 %collective-permute-start.3 = (bf16[512,768]{1,0:T(8,128)(2,1)S(1)}, bf16[512,768]{1,0:T(8,128)(2,1)S(1)}, u32[]{:S(2)}, u32[]{:S(2)}) collective-permute-start(bf16[512,768]{1,0:T(8,128)(2,1)S(1)} %fusion.38), channel_id=1, source_target_pairs={{0,4},{4,0},{1,5},{5,1},{2,6},{6,2},{3,7},{7,3},{8,12},{12,8},{9,1... | collective-permute-start | bytes 2359304 | tf_op jit(solution)/shard_map/ppermute | solution.py:368
  232.1 19.0 %collective-permute-start.1 = (bf16[512,768]{1,0:T(8,128)(2,1)S(1)}, bf16[512,768]{1,0:T(8,128)(2,1)S(1)}, u32[]{:S(2)}, u32[]{:S(2)}) collective-permute-start(bf16[512,768]{1,0:T(8,128)(2,1)S(1)} %get-tuple-element.90), channel_id=1, source_target_pairs={{0,4},{4,0},{1,5},{5,1},{2,6},{6,2},{3,7},{7,3},{8,12},{12,8},{9,1... | collective-permute-start | bytes 2359304 | tf_op jit(solution)/shard_map/ppermute | solution.py:350
  271.0 18.0 %collective-permute-start.2 = (bf16[512,768]{1,0:T(8,128)(2,1)S(1)}, bf16[512,768]{1,0:T(8,128)(2,1)S(1)}, u32[]{:S(2)}, u32[]{:S(2)}) collective-permute-start(bf16[512,768]{1,0:T(8,128)(2,1)S(1)} %fusion.32), channel_id=1, source_target_pairs={{0,4},{4,0},{1,5},{5,1},{2,6},{6,2},{3,7},{7,3},{8,12},{12,8},{9,1... | collective-permute-start | bytes 2359304 | tf_op jit(solution)/shard_map/ppermute | solution.py:368
  295.6 26.1 %copy-start.8 = (f32[512,768]{1,0:T(8,128)}, f32[512,768]{1,0:T(8,128)S(1)}, u32[]{:S(2)}) copy-start(f32[512,768]{1,0:T(8,128)S(1)} %get-tuple-element.96) | copy-start | bytes 4718596
  295.6 111.1 %reduce-scatter.13.cloned.1.call-start = ((), (), s32[]{:S(2)}) async-start(), calls=%async_computation.13 | async-start | bytes 5898240 | tf_op jit(solution)/shard_map/reduce_scatter | solution.py:433
  357.8 99.4 %reduce-scatter.15.cloned.1.call-start = ((), (), s32[]{:S(2)}) async-start(), calls=%async_computation.14 | async-start | bytes 5898240 | tf_op jit(solution)/shard_map/reduce_scatter | solution.py:433
  358.6 163.6 %reduce-scatter.17.cloned.1.call-start = ((), (), s32[]{:S(2)}) async-start(), calls=%async_computation.16 | async-start | bytes 1769472 | tf_op jit(solution)/shard_map/reduce_scatter | solution.py:427
  411.0 36.4 %collective-permute-start.4 = (bf16[1536,512]{1,0:T(8,128)(2,1)}, bf16[1536,512]{1,0:T(8,128)(2,1)}, u32[]{:S(2)}, u32[]{:S(2)}) collective-permute-start(bf16[1536,512]{1,0:T(8,128)(2,1)} %pad_maximum_fusion.2), channel_id=1, source_target_pairs={{0,1},{1,0},{2,3},{3,2},{4,5},{5,4},{6,7},{7,6},{8,9},{9,8},{10,11... | collective-permute-start | bytes 4718600 | tf_op jit(solution)/shard_map/ppermute | solution.py:468
  417.6 154.9 %reduce-scatter.25.cloned.1.call-start = ((), (), s32[]{:S(2)}) async-start(), calls=%async_computation.20 | async-start | bytes 4423680
  522.1 71.9 %reduce-scatter.19.cloned.1.call-start = ((), (), s32[]{:S(2)}) async-start(), calls=%async_computation.17 | async-start | bytes 245760 | tf_op jit(solution)/shard_map/reduce_scatter | solution.py:428
  522.7 101.0 %reduce-scatter.23.cloned.1.call-start = ((), (), s32[]{:S(2)}) async-start(), calls=%async_computation.19 | async-start | bytes 1474560 | tf_op jit(solution)/shard_map/reduce_scatter | solution.py:438
  525.3 129.1 %reduce-scatter.21.cloned.1.call-start = ((), (), s32[]{:S(2)}) async-start(), calls=%async_computation.18 | async-start | bytes 1474560 | tf_op jit(solution)/shard_map/reduce_scatter | solution.py:438
  527.7 190.5 %all-gather.17.cloned.1.call-start = ((), (), s32[]{:S(2)}) async-start(), calls=%async_computation.15 | async-start | bytes 3932160 | tf_op jit(solution)/shard_map/all_gather | solution.py:484
  531.1 209.2 %reduce-scatter.27.cloned.1.call-start = ((), (), s32[]{:S(2)}) async-start(), calls=%async_computation.21 | async-start | bytes 614400
  623.7 123.6 %copy-start.17 = (bf16[2048,768]{1,0:T(8,128)(2,1)S(1)}, bf16[2048,768]{1,0:T(8,128)(2,1)}, u32[]{:S(2)}) copy-start(bf16[2048,768]{1,0:T(8,128)(2,1)} %all-gather.15.cloned.1.call-done) | copy-start | bytes 9437188
  (42 other events, 304.0 us)
Sparse Core Ops, SparseCore 0:
  10.9 51.4 all-gather.6
  64.0 29.5 all-gather.8
  95.8 52.4 all-gather.10
  151.1 51.9 all-gather.12
  295.7 62.0 all-gather.14
  360.2 46.4 reduce-scatter.12
  409.4 47.8 reduce-scatter.14
  460.6 38.4 reduce-scatter.16
  522.2 50.1 reduce-scatter.24
  574.6 19.3 reduce-scatter.18
  596.3 27.3 reduce-scatter.22
  626.5 27.8 reduce-scatter.20
  656.0 62.2 all-gather.16
  720.4 19.8 reduce-scatter.26
